TPU v7x, 256 devices: a whole 4x4x8 slice. The times are simulated.
256 devices in a mesh: row: 16 (over z, y_lo), col: 16 (over y_hi, x, core).
Axes of the slice: x: 4, y: 4 (y_hi: 2, y_lo: 2; y = y_hi * 2 + y_lo), z: 8, core: 2. Of those that a mesh axis runs over, the one named last changes fastest.
Arguments:
- pair_rep: bfloat16 [1024, 1024, 128], P('row', 'col'), may hold values from -6 to 6
- in_gain: float32 [128], replicated, may hold values from 0.5 to 1.5
- proj_weight: bfloat16 [128, 512], replicated, may hold values from -0.5 to 0.5
- gate_weight: bfloat16 [128, 128], replicated, may hold values from -0.5 to 0.5
- out_gain: float32 [128], replicated, may hold values from 0.5 to 1.5
- out_weight: bfloat16 [128, 128], replicated, may hold values from -0.5 to 0.5
Outputs:
- update: bfloat16 [1024, 1024, 128], P('row', 'col')
All inputs are finite; a program needn't handle non-finite values.
Results may differ from a plain program's by a relative error of at most 0.0078.
Values may be sent and summed in bfloat16 or wider, within the bound.
A program may use at most 192 MiB of HBM per device.

v0:
```python
import jax
import jax.numpy as jnp
from jax import lax
from jax.sharding import PartitionSpec as P

EPSILON = 1e-05


def layer_norm(values, gain_vec):
    chan_mean = jnp.mean(values, axis=-1, keepdims=True)
    centred = values - chan_mean
    chan_var = jnp.mean(centred * centred, axis=-1, keepdims=True)
    return centred * lax.rsqrt(chan_var + EPSILON) * gain_vec


def gated_half(normed, weights, hidden):
    projected = jnp.dot(normed, weights, preferred_element_type=jnp.float32)
    return (jax.nn.sigmoid(projected[..., hidden:]) * projected[..., :hidden]).astype(jnp.bfloat16)


def shards(pair_rep, in_gain, proj_weight, gate_weight, out_gain, out_weight):
    hidden = out_weight.shape[0]
    normed = layer_norm(pair_rep.astype(jnp.float32), in_gain).astype(jnp.bfloat16)
    left_tile = gated_half(normed, proj_weight[:, : 2 * hidden], hidden)
    right_tile = gated_half(normed, proj_weight[:, 2 * hidden :], hidden)
    right_all = lax.all_gather(right_tile, "row", axis=0, tiled=True)
    partial_terms = jnp.einsum(
        "ikh,jkh->ijh", left_tile, right_all, preferred_element_type=jnp.float32
    )
    tri_sum = lax.psum_scatter(partial_terms, "col", scatter_dimension=1, tiled=True)
    tri_normed = layer_norm(tri_sum, out_gain).astype(jnp.bfloat16)
    gate = jax.nn.sigmoid(jnp.dot(normed, gate_weight, preferred_element_type=jnp.float32))
    return (gate * jnp.dot(tri_normed, out_weight, preferred_element_type=jnp.float32)).astype(
        jnp.bfloat16
    )


def solution(mesh):
    return jax.shard_map(
        shards,
        mesh=mesh,
        in_specs=(P("row", "col", None), P(), P(), P(), P(), P()),
        out_specs=P("row", "col", None),
        check_vma=False,
    )
```

profile of v0, /device:TPU:1, one launch (start us, length us, event | category | flops | bytes accessed | tf_op | source)
XLA Modules:
  0.0 743.0 jit_solution(15137378593365117162)
XLA Ops:
  6.5 0.0 copy-start
  6.5 0.0 copy-start.1
  6.5 0.0 copy-start.5
  6.5 0.0 copy-start.4
  6.5 0.0 all-gather.2.cloned.1.call-start
  6.6 1.9 convert_reduce_fusion
  8.5 2.3 fusion.2
  10.9 0.0 copy-done.1
  10.9 0.0 copy-done.5
  10.9 0.0 copy-done.4
  10.9 1.3 fusion.16
  12.2 1.5 fusion.9
  13.7 0.0 all-gather.2.cloned.1.call-update
  13.8 0.2 reduce-scatter.2.cloned.1.call-start
  14.0 1.3 fusion.14
  15.3 1.5 fusion.5
  16.8 3.9 copy.23
  20.8 347.9 %all-gather.2.cloned.1.call-done = bf16[1024,64,128]{2,1,0:T(8,128)(2,1)} async-done(((bf16[64,64,128]{2,1,0:T(8,128)(2,1)}), bf16[1024,64,128]{2,1,0:T(8,128)(2,1)}) %all-gather.2.cloned.1.call-update) | async-done | bytes 16777232 | tf_op jit(solution)/shard_map/all_gather | solution.py:26
  368.7 45.5 %copy.22 = bf16[1024,64,128]{1,0,2:T(8,128)(2,1)} copy(bf16[1024,64,128]{2,1,0:T(8,128)(2,1)} %all-gather.2.cloned.1.call-done) | data formatting | bytes 33554432 | tf_op jit(solution)/shard_map/all_gather | solution.py:26
  414.2 24.8 %convolution_bitcast_fusion = f32[64,1024,128]{1,0,2:T(8,128)} fusion(bf16[1024,64,128]{1,0,2:T(8,128)(2,1)} %copy.22, bf16[64,64,128]{1,0,2:T(8,128)(2,1)S(1)} %copy.23), kind=kOutput, calls=%fused_computation | convolution fusion | flops 1073741824 | bytes 51380224 | tf_op jit(solution)/shard_map/ikh,jkh->ijh/dot_general | solution.py:27
  438.9 32.6 %copy.24 = f32[64,1024,128]{2,0,1:T(8,128)} copy(f32[64,1024,128]{1,0,2:T(8,128)} %convolution_bitcast_fusion) | data formatting | bytes 67108864 | tf_op jit(solution)/shard_map/ikh,jkh->ijh/transpose | solution.py:27
  471.6 0.0 reduce-scatter.2.cloned.1.call-update
  471.6 0.0 copy-done
  471.6 2.5 fusion.18
  474.1 0.0 copy-start.6
  474.1 254.3 %reduce-scatter.2.cloned.1.call-done = f32[64,64,128]{2,0,1:T(8,128)} async-done(((f32[64,1024,128]{2,0,1:T(8,128)}), f32[64,64,128]{2,0,1:T(8,128)}) %reduce-scatter.2.cloned.1.call-update) | async-done | bytes 2097168 | tf_op jit(solution)/shard_map/reduce_scatter | solution.py:30
  728.4 0.0 copy-start.2
  728.4 2.4 reduce_sum.38
  730.8 0.1 copy.25
  730.8 0.1 copy.26
  730.9 0.0 copy-done.2
  730.9 1.3 multiply_reduce_fusion
  732.3 0.0 copy-start.7
  732.3 0.1 copy.27
  732.4 0.1 copy.28
  732.4 0.0 copy-done.6
  732.5 0.0 copy-start.3
  732.5 1.2 multiply_convert_fusion.1
  733.7 0.0 copy-done.7
  733.7 0.3 copy-done.3
  734.1 2.2 multiply_convert_fusion
  (4 shorter events, 0.0 us)
Async XLA Ops:
  6.5 465.0 %copy-start = (bf16[128,128]{1,0:T(8,128)(2,1)S(1)}, bf16[128,128]{1,0:T(8,128)(2,1)}, u32[]{:S(2)}) copy-start(bf16[128,128]{1,0:T(8,128)(2,1)} %param.9) | copy-start | bytes 98308
  6.5 4.4 copy-start.1
  6.5 4.4 copy-start.5
  6.5 4.4 copy-start.4
  6.5 362.2 %all-gather.2.cloned.1.call-start = ((), (), s32[]{:S(2)}) async-start(), calls=%async_computation.1 | async-start | bytes 17825792 | tf_op jit(solution)/shard_map/all_gather | solution.py:26
  13.8 714.6 %reduce-scatter.2.cloned.1.call-start = ((), (), s32[]{:S(2)}) async-start(), calls=%async_computation.2 | async-start | bytes 35651584 | tf_op jit(solution)/shard_map/reduce_scatter | solution.py:30
  474.1 258.3 %copy-start.6 = (f32[128]{0:T(128)S(1)}, f32[128]{0:T(128)}, u32[]{:S(2)}) copy-start(f32[128]{0:T(128)} %param.10) | copy-start | bytes 1540
  728.4 2.5 copy-start.2
  732.3 1.5 copy-start.7
  732.5 1.6 copy-start.3
Sparse Core Ops, SparseCore 0:
  13.9 354.7 all-gather.1
  471.7 256.6 reduce-scatter.1
where the time goes:
time: 747 us; the launch traced here: 743 us
  waiting for transfers between devices  602 us (81%)
  local copies, waits for them, and re-layouts  82.7 us (11%)
  matrix products  32 us (4%)
  between operations  13.6 us (2%)
  other arithmetic  12.3 us (2%)
    all_gather x1, waiting for transfers between devices, shards(): right_all = lax.all_gather(right_tile, 'row', axis=0, tiled=True)  348 us
    reduce_scatter x1, waiting for transfers between devices, shards(): lax.psum_scatter(partial_terms, 'col', scatter_dimension=1, tiled=True)  254 us
    all_gather x1, local copies, waits for them, and re-layouts, shards(): right_all = lax.all_gather(right_tile, 'row', axis=0, tiled=True)  45.5 us
    transpose x1, local copies, waits for them, and re-layouts, shards(): jnp.einsum('ikh,jkh->ijh', left_tile, right_all, preferred_element_type=j...  32.6 us
    dot_general x1, matrix products, shards(): jnp.einsum('ikh,jkh->ijh', left_tile, right_all, preferred_element_type=j...  24.8 us
  transfers between devices with their start and end apart: 2, of which 2 were waited for; matrix products, arithmetic and copies ran while one was open for 1% of the time, Pallas kernels for 0%

commit v1 on v0

v1 whole, which is shorter than its diff:
```python
import functools

import jax
import jax.numpy as jnp
from jax import lax
from jax.experimental import pallas as pl
from jax.experimental.pallas import tpu as pltpu
from jax.sharding import PartitionSpec as P

EPSILON = 1e-05
MESH = pl.DeviceIdType.MESH
F32, BF16 = jnp.float32, jnp.bfloat16

CHUNKS = 2
ROWS = 32 // CHUNKS
NT = (((1,), (1,)), ((), ()))
TN = (((0,), (0,)), ((), ()))


def sigmoid(values):
    return 0.5 * jnp.tanh(0.5 * values) + 0.5


def kernel(
    x_ref, in_gain_ref, proj_ref, gate_w_ref, out_gain_ref, out_w_ref, o_ref,
    normed, other, wide, right_send, left_send, right_buf, left_buf,
    tri_send, tri_buf, gates, result, weights_t, gain_cols,
    ready, swap_sems, right_sems, fwd_sems, left_sems, tri_sems, out_sems, local_sems,
):
    row, col = lax.axis_index("row"), lax.axis_index("col")
    z, y_lo = row // 2, lax.rem(row, 2)
    pair, core = col // 2, lax.rem(col, 2)
    y_hi, x = pair // 4, lax.rem(pair, 4)
    me = row * 8 + pair
    sibling = (row, pair * 2 + 1 - core)

    def shifted(dz, dyl, dyh, dx):
        row2 = lax.rem(z + dz, 8) * 2 + lax.rem(y_lo + dyl, 2)
        pair2 = lax.rem(y_hi + dyh, 2) * 4 + lax.rem(x + dx, 4)
        return row2, pair2

    def shifted_all(step):
        dz, rest = lax.rem(step, 8), step // 8
        return shifted(dz, lax.rem(rest // 4, 2), rest // 8, lax.rem(rest, 4))

    barrier = pltpu.get_barrier_semaphore()

    def greet(device):
        pl.semaphore_signal(barrier, inc=1, device_id=device, device_id_type=MESH)

    def greet_z(step, carry):
        row2, pair2 = shifted(step, 0, 0, 0)
        greet((row2, pair2 * 2 + core))
        return carry

    def greet_plane(step, carry):
        row2, pair2 = shifted(0, lax.rem(step // 4, 2), step // 8, lax.rem(step, 4))
        greet((row2, pair2 * 2 + core))
        return carry

    greet(sibling)
    lax.fori_loop(1, 16, greet_plane, 0)
    lax.fori_loop(1, 8, greet_z, 0)

    gain = in_gain_ref[...]

    def norm_rows(values):
        values = values.astype(F32).reshape(-1, 128)
        mean = jnp.mean(values, axis=-1, keepdims=True)
        centred = values - mean
        var = jnp.mean(centred * centred, axis=-1, keepdims=True)
        return (centred * lax.rsqrt(var + EPSILON) * gain).astype(BF16)

    def norm_away(step, carry):
        first = pl.multiple_of(step * 4, 4)
        other[pl.ds(first, 4)] = norm_rows(x_ref[pl.ds(32 * (1 - core) + first, 4)]).reshape(4, 64, 128)
        return carry

    def norm_own(step, carry):
        first = pl.multiple_of(step * 4, 4)
        normed[pl.ds(first, 4), pl.ds(pl.multiple_of(64 * core, 64), 64), :] = norm_rows(
            x_ref[pl.ds(32 * core + first, 4)]
        ).reshape(4, 64, 128)
        return carry

    lax.fori_loop(0, 8, norm_away, 0)
    pl.semaphore_wait(barrier, 23)
    swap = pltpu.make_async_remote_copy(
        src_ref=other,
        dst_ref=normed.at[:, pl.ds(pl.multiple_of(64 * core, 64), 64), :],
        send_sem=swap_sems.at[0], recv_sem=swap_sems.at[1],
        device_id=sibling, device_id_type=MESH,
    )
    swap.start()

    def ready_z(step, carry):
        row2, pair2 = shifted(step, 0, 0, 0)
        pl.semaphore_signal(
            ready, inc=1, device_id=(row2, pair2 * 2 + core), device_id_type=MESH
        )
        return carry

    lax.fori_loop(1, 8, ready_z, 0)
    lax.fori_loop(0, 8, norm_own, 0)
    weights_t[...] = proj_ref[...].astype(F32).T.astype(BF16)
    gain_cols[...] = jnp.broadcast_to(out_gain_ref[...], (128, 128)).T
    swap.wait()

    def project(first_row, send, chunks):
        half = weights_t[first_row : first_row + 256, :]

        def some(step, carry):
            first = pl.multiple_of(step * 4, 4)
            rows = normed[pl.ds(first, 4)].reshape(512, 128)
            both = lax.dot_general(half, rows, NT, preferred_element_type=F32)
            side = sigmoid(both[128:]) * both[:128]
            for i in range(4):
                wide[pl.ds(first + i, 128, stride=32), :] = side[:, i * 128 : (i + 1) * 128]
            return carry

        lax.fori_loop(0, 8, some, 0)
        size = 32 // chunks

        def narrow(step, carry):
            block = wide[pl.ds(pl.multiple_of(step * 128, 128), 128), :].astype(BF16)
            block = block.reshape(4, chunks, size, 128)
            for c in range(chunks):
                send[c, pl.ds(step * 4, 4)] = block[:, c]
            return carry

        lax.fori_loop(0, 32, narrow, 0)

    project(256, right_send, 1)
    pl.semaphore_wait(ready, 7)

    def send_right(step, carry):
        row2, pair2 = shifted_all(step)
        pltpu.make_async_remote_copy(
            src_ref=right_send.at[0, row2 * 8 + pair2],
            dst_ref=right_buf.at[row, core, pair],
            send_sem=right_sems.at[0], recv_sem=right_sems.at[1],
            device_id=(row2, pair2 * 2 + core), device_id_type=MESH,
        ).start()
        return carry

    lax.fori_loop(1, 128, send_right, 0)
    own_right = pltpu.make_async_copy(
        right_send.at[0, me], right_buf.at[row, core, pair], local_sems.at[0]
    )
    own_right.start()

    project(0, left_send, CHUNKS)
    own_left = []
    for c in range(CHUNKS):

        def send_left(step, carry, c=c):
            row2, pair2 = shifted_all(step)
            pltpu.make_async_remote_copy(
                src_ref=left_send.at[c, row2 * 8 + pair2],
                dst_ref=left_buf.at[c, row, pair],
                send_sem=left_sems.at[0, c], recv_sem=left_sems.at[1, c],
                device_id=(row2, pair2 * 2 + core), device_id_type=MESH,
            ).start()
            return carry

        lax.fori_loop(1, 128, send_left, 0)
        own = pltpu.make_async_copy(
            left_send.at[c, me], left_buf.at[c, row, pair], local_sems.at[1 + c]
        )
        own.start()
        own_left.append(own)

    def gate_rows(step, carry):
        first = pl.multiple_of(step * 4, 4)
        rows = normed[pl.ds(first, 4)].reshape(512, 128)
        gates[pl.ds(first, 4)] = sigmoid(
            jnp.dot(rows, gate_w_ref[...], preferred_element_type=F32)
        ).reshape(4, 128, 128)
        return carry

    lax.fori_loop(0, 8, gate_rows, 0)

    def wait_all(refs, sems):
        copy = pltpu.make_async_remote_copy(
            src_ref=refs.at[pl.ds(0, 127)], dst_ref=refs.at[pl.ds(0, 127)],
            send_sem=sems[0], recv_sem=sems[1], device_id=sibling, device_id_type=MESH,
        )
        return copy

    own_right.wait()
    wait_all(right_send.at[0], (right_sems.at[0], right_sems.at[1])).wait_recv()
    forward = pltpu.make_async_remote_copy(
        src_ref=right_buf.at[:, core], dst_ref=right_buf.at[:, core],
        send_sem=fwd_sems.at[0], recv_sem=fwd_sems.at[1],
        device_id=sibling, device_id_type=MESH,
    )
    forward.start()
    forward.wait()

    for c in range(CHUNKS):
        own_left[c].wait()
        wait_all(left_send.at[c], (left_sems.at[0, c], left_sems.at[1, c])).wait_recv()

        def columns(step, carry, c=c):
            n = lax.rem(step + pair // 2, 4)
            total = None
            for k in range(4):
                left = jnp.concatenate(
                    [left_buf[c, :, 2 * k + s].reshape(16 * ROWS, 128) for s in range(2)], axis=-1
                )
                right = jnp.concatenate(
                    [right_buf[pl.ds(4 * n, 4), :, 2 * k + s].reshape(256, 128) for s in range(2)],
                    axis=-1,
                )
                term = lax.dot_general(left, right, NT, preferred_element_type=F32)
                total = term if total is None else total + term
            tiles = total.astype(BF16).reshape(16, ROWS, 256)
            for s in range(2):
                tri_send[c, :, 2 * n + s] = tiles[:, :, s * 128 : (s + 1) * 128]

            def send_tri(part, inner):
                dz, rest = lax.rem(part, 8), part // 8
                row2 = lax.rem(z + dz, 8) * 2 + lax.rem(y_lo + rest // 2, 2)
                pair2 = 2 * n + lax.rem(pair + lax.rem(rest, 2), 2)
                away = row2 * 8 + pair2 != me

                @pl.when(away)
                def _():
                    pltpu.make_async_remote_copy(
                        src_ref=tri_send.at[c, row2, pair2],
                        dst_ref=tri_buf.at[c, me],
                        send_sem=tri_sems.at[0, c], recv_sem=tri_sems.at[1, c],
                        device_id=(row2, pair2 * 2 + core), device_id_type=MESH,
                    ).start()

                return inner

            lax.fori_loop(0, 32, send_tri, 0)
            return carry

        lax.fori_loop(0, 4, columns, 0)
        own = pltpu.make_async_copy(
            tri_send.at[c, row, pair], tri_buf.at[c, me], local_sems.at[1 + CHUNKS + c]
        )
        own.start()
        own.wait()

    for c in range(CHUNKS):
        wait_all(left_send.at[c], (tri_sems.at[0, c], tri_sems.at[1, c])).wait_recv()

        def channel_sum(first, size):
            def add(h, acc):
                return acc + tri_buf[c, h].astype(F32)

            return lax.fori_loop(0, 128, add, jnp.zeros((ROWS, 128), F32), unroll=8)

        mean = channel_sum(0, 128) * (1.0 / 128.0)

        def add_square(h, acc, c=c, mean=mean):
            centred = tri_buf[c, h].astype(F32) - mean
            wide[pl.ds(pl.multiple_of(h * ROWS, ROWS), ROWS), :] = centred
            return acc + centred * centred

        var = lax.fori_loop(0, 128, add_square, jnp.zeros((ROWS, 128), F32), unroll=8) * (1.0 / 128.0)
        scale = lax.rsqrt(var + EPSILON)
        scales = gain_cols[...]
        for i in range(ROWS):
            tile = wide[pl.ds(i, 128, stride=ROWS), :] * scale[i : i + 1, :] * scales
            projected = lax.dot_general(
                tile.astype(BF16), out_w_ref[...], TN, preferred_element_type=F32
            )
            result[c * ROWS + i] = (gates[c * ROWS + i] * projected).astype(BF16)

    keep = pltpu.make_async_copy(
        result.at[:, pl.ds(pl.multiple_of(64 * core, 64), 64), :],
        o_ref.at[pl.ds(32 * core, 32)], local_sems.at[1 + 2 * CHUNKS],
    )
    keep.start()
    give = pltpu.make_async_remote_copy(
        src_ref=result.at[:, pl.ds(pl.multiple_of(64 * (1 - core), 64), 64), :],
        dst_ref=o_ref.at[pl.ds(32 * core, 32)],
        send_sem=out_sems.at[0], recv_sem=out_sems.at[1],
        device_id=sibling, device_id_type=MESH,
    )
    give.start()
    wait_all(right_send.at[0], (right_sems.at[0], right_sems.at[1])).wait_send()
    for c in range(CHUNKS):
        wait_all(left_send.at[c], (left_sems.at[0, c], left_sems.at[1, c])).wait_send()
        wait_all(left_send.at[c], (tri_sems.at[0, c], tri_sems.at[1, c])).wait_send()
    keep.wait()
    give.wait()


def shards(pair_rep, in_gain, proj_weight, gate_weight, out_gain, out_weight):
    vmem = pl.BlockSpec(memory_space=pltpu.VMEM)
    return pl.pallas_call(
        kernel,
        out_shape=jax.ShapeDtypeStruct((64, 64, 128), BF16),
        in_specs=[vmem] * 6,
        out_specs=pl.BlockSpec(memory_space=pl.ANY),
        scratch_shapes=[
            pltpu.VMEM((32, 128, 128), BF16),
            pltpu.VMEM((32, 64, 128), BF16),
            pltpu.VMEM((128 * 32, 128), F32),
            pltpu.VMEM((1, 128, 32, 128), BF16),
            pltpu.VMEM((CHUNKS, 128, ROWS, 128), BF16),
            pltpu.VMEM((16, 2, 8, 32, 128), BF16),
            pltpu.VMEM((CHUNKS, 16, 8, ROWS, 128), BF16),
            pltpu.VMEM((CHUNKS, 16, 8, ROWS, 128), BF16),
            pltpu.VMEM((CHUNKS, 128, ROWS, 128), BF16),
            pltpu.VMEM((32, 128, 128), F32),
            pltpu.VMEM((32, 128, 128), BF16),
            pltpu.VMEM((512, 128), BF16),
            pltpu.VMEM((128, 128), F32),
            pltpu.SemaphoreType.REGULAR,
            pltpu.SemaphoreType.DMA((2,)),
            pltpu.SemaphoreType.DMA((2,)),
            pltpu.SemaphoreType.DMA((2,)),
            pltpu.SemaphoreType.DMA((2, CHUNKS)),
            pltpu.SemaphoreType.DMA((2, CHUNKS)),
            pltpu.SemaphoreType.DMA((2,)),
            pltpu.SemaphoreType.DMA((2 + 2 * CHUNKS,)),
        ],
        compiler_params=pltpu.CompilerParams(
            collective_id=0, has_side_effects=True, vmem_limit_bytes=40 * 2**20
        ),
    )(
        pair_rep, in_gain.reshape(1, 128), proj_weight, gate_weight,
        out_gain.reshape(1, 128), out_weight,
    )


def solution(mesh):
    return jax.shard_map(
        shards,
        mesh=mesh,
        in_specs=(P("row", "col", None), P(), P(), P(), P(), P()),
        out_specs=P("row", "col", None),
        check_vma=False,
    )
```

time: 747 us -> 95.8 us (0.13)
  waiting for transfers between devices: 602 us -> 0 us
  Pallas kernels: 0 us -> 90.2 us
  local copies, waits for them, and re-layouts: 82.7 us -> 5.28 us
  matrix products: 32 us -> 0 us
  between operations: 13.6 us -> 0.02 us
  other arithmetic: 12.3 us -> 0 us
    all_gather x1 -> x0, waiting for transfers between devices: 348 us -> none  [shards(): right_all = lax.all_gather(right_tile, 'row', axis=0, tiled=True)]
    reduce_scatter x1 -> x0, waiting for transfers between devices: 254 us -> none  [shards(): lax.psum_scatter(partial_terms, 'col', scatter_dimension=1, tiled=True)]
    pallas_call x0 -> x1, Pallas kernels: none -> 90.2 us  [shards(): pl.pallas_call(kernel, out_shape=jax.ShapeDtypeStruct((64, 64, 128), BF16...]
    all_gather x1 -> x0, local copies, waits for them, and re-layouts: 45.5 us -> none  [shards(): right_all = lax.all_gather(right_tile, 'row', axis=0, tiled=True)]
    transpose x1 -> x0, local copies, waits for them, and re-layouts: 32.6 us -> none  [shards(): jnp.einsum('ikh,jkh->ijh', left_tile, right_all, preferred_element_type=j...]
    dot_general x5 -> x0, matrix products: 32 us -> none  [the longest x1 24.8 us: shards(): jnp.einsum('ikh,jkh->ijh', left_tile, right_all, preferred_element_type=j...]
    reduce_sum x4 -> x0, other arithmetic: 7.93 us -> none  [the longest x2 4.28 us: layer_norm(): chan_mean = jnp.mean(values, axis=-1, keepdims=True)]
  transfers between devices with their start and end apart: 2 -> 0, of which waited for: 2 -> 0; matrix products, arithmetic and copies ran while one was open for 1% -> 0% of each run, Pallas kernels for 0% -> 0%
where the time goes in v1:
time: 95.8 us; the launch traced here: 95.5 us
  Pallas kernels  90.2 us (94%)
  local copies, waits for them, and re-layouts  5.28 us (6%)
    pallas_call x1, Pallas kernels, shards(): pl.pallas_call(kernel, out_shape=jax.ShapeDtypeStruct((64, 64, 128), BF16...  90.2 us
    unnamed x13, local copies, waits for them, and re-layouts  5.28 us

profile of v1, /device:TPU:1, one launch (start us, length us, event | category | flops | bytes accessed | tf_op | source)
XLA Modules:
  0.0 95.5 jit_solution(7667164298796869963)
XLA Ops:
  0.0 0.0 copy-start.4
  0.0 0.0 copy-start.5
  0.0 0.7 copy-done.4
  0.7 0.0 copy-done.5
  0.7 0.0 copy-start
  0.7 1.2 %copy-done = bf16[64,64,128]{2,1,0:T(8,128)(2,1)S(1)} copy-done((bf16[64,64,128]{2,1,0:T(8,128)(2,1)S(1)}, bf16[64,64,128]{2,1,0:T(8,128)(2,1)}, u32[]{:S(2)}) %copy-start) | copy-done | bytes 1048600
  1.9 0.0 copy-start.1
  1.9 0.9 copy-done.1
  2.8 0.0 copy-start.2
  2.8 0.8 copy-done.2
  3.6 0.0 copy-start.3
  3.6 0.8 copy-done.3
  4.3 90.2 %shard_map.64 = bf16[64,64,128]{2,1,0:T(8,128)(2,1)S(1)} custom-call(bf16[64,64,128]{2,1,0:T(8,128)(2,1)S(1)} %copy-done, f32[1,128]{1,0:T(1,128)S(1)} %bitcast.2, bf16[128,512]{1,0:T(8,128)(2,1)S(1)} %copy-done.1, bf16[128,128]{1,0:T(8,128)(2,1)S(1)} %copy-done.2, f32[1,128]{1,0:T(1,128)S(1)} %bitcast.3, bf16[128,128]{1,0:T(8,128)(2,1)S(1)} %copy-done.3), custom_call_target="tpu_custom_call" | custom-call | tf_op jit(solution)/shard_map/pallas_call | solution.py:296
  94.5 1.0 %copy.8 = bf16[64,64,128]{2,1,0:T(8,128)(2,1)} copy(bf16[64,64,128]{2,1,0:T(8,128)(2,1)S(1)} %shard_map.64) | data formatting | bytes 2097152
Async XLA Ops:
  0.0 0.7 copy-start.4
  0.0 0.7 copy-start.5
  0.7 1.2 %copy-start = (bf16[64,64,128]{2,1,0:T(8,128)(2,1)S(1)}, bf16[64,64,128]{2,1,0:T(8,128)(2,1)}, u32[]{:S(2)}) copy-start(bf16[64,64,128]{2,1,0:T(8,128)(2,1)} %x_ref.1) | copy-start | bytes 3145732
  1.9 0.9 copy-start.1
  2.8 0.8 copy-start.2
  3.6 0.8 copy-start.3

commit v2 on v1

v2 whole, which is shorter than its diff:
```python
import jax
import jax.numpy as jnp
from jax import lax
from jax.experimental import pallas as pl
from jax.experimental.pallas import tpu as pltpu
from jax.sharding import PartitionSpec as P

EPSILON = 1e-05
MESH = pl.DeviceIdType.MESH
F32, BF16 = jnp.float32, jnp.bfloat16

CHUNKS = 2
ROWS = 32 // CHUNKS
NT = (((1,), (1,)), ((), ()))
TN = (((0,), (0,)), ((), ()))


def sigmoid(values):
    return 0.5 * jnp.tanh(0.5 * values) + 0.5


def kernel(
    x_hbm, in_gain_hbm, proj_hbm, gate_w_hbm, out_gain_hbm, out_w_hbm, o_ref,
    x_ref, in_gain_ref, proj_ref, gate_w_ref, out_gain_ref, out_w_ref,
    normed, other, wide, right_send, left_send, right_buf, left_buf,
    tri_send, tri_buf, gates, result, weights_t, gain_cols,
    ready, ready_core, load_sems, swap_sems, right_sems, own_sems, fwd_sems,
    left_sems, tri_sems, out_sems,
):
    row, col = lax.axis_index("row"), lax.axis_index("col")
    z, y_lo = row // 2, lax.rem(row, 2)
    pair, core = col // 2, lax.rem(col, 2)
    y_hi, x = pair // 4, lax.rem(pair, 4)
    place = y_lo * 8 + pair
    up = 1 - core
    me = lax.rem(z + 8 - core, 8) * 16 + place
    sibling = (row, pair * 2 + 1 - core)
    partner = (lax.rem(z + 7 + 2 * up, 8) * 2 + y_lo, pair * 2 + 1 - core)

    loads = [
        pltpu.make_async_copy(src, dst, load_sems.at[i])
        for i, (src, dst) in enumerate((
            (x_hbm, x_ref), (in_gain_hbm, in_gain_ref), (proj_hbm, proj_ref),
            (gate_w_hbm, gate_w_ref), (out_gain_hbm, out_gain_ref), (out_w_hbm, out_w_ref),
        ))
    ]
    for load in loads:
        load.start()

    def plane_at(step):
        y_lo2 = lax.rem(y_lo + lax.rem(step // 4, 2), 2)
        pair2 = lax.rem(y_hi + step // 8, 2) * 4 + lax.rem(x + lax.rem(step, 4), 4)
        return y_lo2, pair2

    barrier = pltpu.get_barrier_semaphore()

    def greet(device):
        pl.semaphore_signal(barrier, inc=1, device_id=device, device_id_type=MESH)

    def greet_z(step, carry):
        greet((lax.rem(z + step, 8) * 2 + y_lo, col))
        return carry

    def greet_plane(step, carry):
        y_lo2, pair2 = plane_at(step)
        greet((z * 2 + y_lo2, pair2 * 2 + core))
        return carry

    lax.fori_loop(1, 8, greet_z, 0)
    lax.fori_loop(1, 16, greet_plane, 0)
    greet(sibling)

    loads[1].wait()
    loads[0].wait()
    gain = in_gain_ref[...]

    def norm_rows(values):
        values = values.astype(F32).reshape(-1, 128)
        mean = jnp.mean(values, axis=-1, keepdims=True)
        centred = values - mean
        var = jnp.mean(centred * centred, axis=-1, keepdims=True)
        return (centred * lax.rsqrt(var + EPSILON) * gain).astype(BF16)

    own_cols = pl.ds(pl.multiple_of(64 * core, 64), 64)
    away_cols = pl.ds(pl.multiple_of(64 * (1 - core), 64), 64)

    def norm_away(step, carry):
        first = pl.multiple_of(step * 4, 4)
        other[pl.ds(first, 4)] = norm_rows(x_ref[pl.ds(32 * (1 - core) + first, 4)]).reshape(4, 64, 128)
        return carry

    def norm_own(step, carry):
        first = pl.multiple_of(step * 4, 4)
        normed[pl.ds(first, 4), own_cols, :] = norm_rows(
            x_ref[pl.ds(32 * core + first, 4)]
        ).reshape(4, 64, 128)
        return carry

    lax.fori_loop(0, 8, norm_away, 0)
    lax.fori_loop(0, 8, norm_own, 0)
    for load in loads[2:]:
        load.wait()
    weights_t[...] = proj_ref[...].astype(F32).T.astype(BF16)
    gain_cols[...] = jnp.broadcast_to(out_gain_ref[...], (128, 128)).T

    pl.semaphore_wait(barrier, 23)
    swaps = []
    for part in range(4):
        swap = pltpu.make_async_remote_copy(
            src_ref=other.at[pl.ds(8 * part, 8)],
            dst_ref=normed.at[pl.ds(8 * part, 8), own_cols, :],
            send_sem=swap_sems.at[0, part], recv_sem=swap_sems.at[1, part],
            device_id=sibling, device_id_type=MESH,
        )
        swap.start()
        swaps.append(swap)

    def ready_z(step, carry):
        pl.semaphore_signal(
            ready, inc=1, device_id=(lax.rem(z + step, 8) * 2 + y_lo, col), device_id_type=MESH
        )
        return carry

    lax.fori_loop(1, 8, ready_z, 0)

    def project(first_row, part):
        half = weights_t[first_row : first_row + 256, :]

        def some(step, carry):
            first = pl.multiple_of(8 * part + step * 4, 4)
            rows = normed[pl.ds(first, 4)].reshape(512, 128)
            both = lax.dot_general(half, rows, NT, preferred_element_type=F32)
            side = sigmoid(both[128:]) * both[:128]
            for i in range(4):
                wide[pl.ds(first + i, 128, stride=32), :] = side[:, i * 128 : (i + 1) * 128]
            return carry

        lax.fori_loop(0, 2, some, 0)

    def toward(up2, dz):
        z2 = lax.rem(z + 8 + (2 * up2 - 1) * dz, 8)
        return z2, lax.rem(z2 + 7 + up2, 8)

    for part in range(4):
        swaps[part].wait()
        project(256, part)
    pl.semaphore_wait(ready, 7)
    pl.semaphore_signal(ready_core, inc=1, device_id=sibling, device_id_type=MESH)
    pl.semaphore_wait(ready_core, 1)

    def send_right(group, carry):
        dz, up2 = 3 - group // 2, lax.rem(up + group + 1, 2)
        z2, cls = toward(up2, dz)

        def narrow(step, inner):
            first = pl.multiple_of(cls * 512 + step * 128, 128)
            right_send[pl.ds(cls * 16 + step * 4, 4)] = (
                wide[pl.ds(first, 128), :].astype(BF16).reshape(4, 32, 128)
            )
            return inner

        lax.fori_loop(0, 4, narrow, 0)

        def send(step, inner):
            y_lo2, pair2 = plane_at(step)

            @pl.when(cls * 16 + y_lo2 * 8 + pair2 != me)
            def _():
                pltpu.make_async_remote_copy(
                    src_ref=right_send.at[cls * 16 + y_lo2 * 8 + pair2],
                    dst_ref=right_buf.at[row, core, pair],
                    send_sem=right_sems.at[4], recv_sem=right_sems.at[dz],
                    device_id=(z2 * 2 + y_lo2, pair2 * 2 + 1 - up2), device_id_type=MESH,
                ).start()

            return inner

        lax.fori_loop(0, 16, send, 0)
        return carry

    lax.fori_loop(0, 8, send_right, 0)
    own_right = pltpu.make_async_copy(
        right_send.at[me], right_buf.at[row, core, pair], own_sems.at[0]
    )
    own_right.start()

    for part in range(4):
        project(0, part)

    def narrow_left(step, carry):
        block = wide[pl.ds(pl.multiple_of(step * 128, 128), 128), :].astype(BF16)
        block = block.reshape(4, CHUNKS, ROWS, 128)
        for c in range(CHUNKS):
            left_send[c, pl.ds(step * 4, 4)] = block[:, c]
        return carry

    lax.fori_loop(0, 32, narrow_left, 0)

    def send_left_chunk(c):
        def send_left(step, carry):
            group = lax.rem(step, 8)
            dz, up2 = 3 - group // 2, lax.rem(up + group + 1, 2)
            z2, cls = toward(up2, dz)
            y_lo2, pair2 = plane_at(step // 8)

            @pl.when(cls * 16 + y_lo2 * 8 + pair2 != me)
            def _():
                pltpu.make_async_remote_copy(
                    src_ref=left_send.at[c, cls * 16 + y_lo2 * 8 + pair2],
                    dst_ref=left_buf.at[c, dz * 2 + y_lo, core, pair],
                    send_sem=left_sems.at[0, c], recv_sem=left_sems.at[1, c],
                    device_id=(z2 * 2 + y_lo2, pair2 * 2 + 1 - up2), device_id_type=MESH,
                ).start()

            return carry

        lax.fori_loop(0, 128, send_left, 0)
        own = pltpu.make_async_copy(
            left_send.at[c, me], left_buf.at[c, y_lo, core, pair], own_sems.at[1 + c]
        )
        own.start()
        return own

    own_left = [send_left_chunk(0)]

    def gate_rows(step, carry):
        first = pl.multiple_of(step * 4, 4)
        rows = normed[pl.ds(first, 4)].reshape(512, 128)
        gates[pl.ds(first, 4)] = sigmoid(
            jnp.dot(rows, gate_w_ref[...], preferred_element_type=F32)
        ).reshape(4, 128, 128)
        return carry

    lax.fori_loop(0, 8, gate_rows, 0)

    def wait_all(refs, count, send_sem, recv_sem):
        return pltpu.make_async_remote_copy(
            src_ref=refs.at[pl.ds(0, count)], dst_ref=refs.at[pl.ds(0, count)],
            send_sem=send_sem, recv_sem=recv_sem, device_id=sibling, device_id_type=MESH,
        )

    forwards = []
    for dz in (3, 2, 1, 0):
        if dz == 0:
            own_right.wait()
        wait_all(right_send, 32 if dz else 31, right_sems.at[4], right_sems.at[dz]).wait_recv()
        source = right_buf.at[pl.ds(2 * lax.rem(z + 8 + (1 - 2 * up) * dz, 8), 2)]
        forward = pltpu.make_async_remote_copy(
            src_ref=source, dst_ref=source,
            send_sem=fwd_sems.at[0, dz], recv_sem=fwd_sems.at[1, dz],
            device_id=partner, device_id_type=MESH,
        )
        forward.start()
        forwards.append(forward)
    for c in range(1, CHUNKS):
        own_left.append(send_left_chunk(c))
    for forward in forwards:
        forward.wait()

    for c in range(CHUNKS):
        own_left[c].wait()
        wait_all(left_send.at[c], 127, left_sems.at[0, c], left_sems.at[1, c]).wait_recv()

        def columns(step, carry, c=c):
            n = lax.rem(step + pair // 2, 4)
            total = None
            for k in range(4):
                left = jnp.concatenate(
                    [left_buf[c, :, :, 2 * k + s].reshape(16 * ROWS, 128) for s in range(2)], axis=-1
                )
                right = jnp.concatenate(
                    [right_buf[pl.ds(4 * n, 4), :, 2 * k + s].reshape(256, 128) for s in range(2)],
                    axis=-1,
                )
                term = lax.dot_general(left, right, NT, preferred_element_type=F32)
                total = term if total is None else total + term
            tiles = total.astype(BF16).reshape(8, 2, ROWS, 256)
            for s in range(2):
                tri_send[c, :, :, 2 * n + s] = tiles[..., s * 128 : (s + 1) * 128]

            def send_tri(part, inner):
                dz, rest = 3 - lax.rem(part, 4), part // 4
                core2, y_lo2 = lax.rem(rest, 2), lax.rem(y_lo + lax.rem(rest // 2, 2), 2)
                pair2 = 2 * n + lax.rem(pair + rest // 4, 2)
                row2 = lax.rem(z + 8 + (1 - 2 * up) * dz, 8) * 2 + y_lo2
                col2 = pair2 * 2 + core2

                @pl.when(row2 * 16 + col2 != row * 16 + col)
                def _():
                    pltpu.make_async_remote_copy(
                        src_ref=tri_send.at[c, dz * 2 + y_lo2, core2, pair2],
                        dst_ref=tri_buf.at[c, me],
                        send_sem=tri_sems.at[0, c], recv_sem=tri_sems.at[1, c],
                        device_id=(row2, col2), device_id_type=MESH,
                    ).start()

                return inner

            lax.fori_loop(0, 32, send_tri, 0)
            return carry

        lax.fori_loop(0, 4, columns, 0)
        own = pltpu.make_async_copy(
            tri_send.at[c, y_lo, core, pair], tri_buf.at[c, me], own_sems.at[1 + CHUNKS + c]
        )
        own.start()
        own.wait()

    outs = []
    for c in range(CHUNKS):
        wait_all(left_send.at[c], 127, tri_sems.at[0, c], tri_sems.at[1, c]).wait_recv()

        def add(h, acc, c=c):
            return acc + tri_buf[c, h].astype(F32)

        mean = lax.fori_loop(0, 128, add, jnp.zeros((ROWS, 128), F32), unroll=8) * (1.0 / 128.0)

        def add_square(h, acc, c=c, mean=mean):
            centred = tri_buf[c, h].astype(F32) - mean
            wide[pl.ds(pl.multiple_of(h * ROWS, ROWS), ROWS), :] = centred
            return acc + centred * centred

        var = lax.fori_loop(0, 128, add_square, jnp.zeros((ROWS, 128), F32), unroll=8) * (1.0 / 128.0)
        scale = lax.rsqrt(var + EPSILON)
        scales = gain_cols[...]
        for i in range(ROWS):
            tile = wide[pl.ds(i, 128, stride=ROWS), :] * scale[i : i + 1, :] * scales
            projected = lax.dot_general(
                tile.astype(BF16), out_w_ref[...], TN, preferred_element_type=F32
            )
            result[c * ROWS + i] = (gates[c * ROWS + i] * projected).astype(BF16)

        rows = pl.ds(c * ROWS, ROWS)
        place_rows = pl.ds(32 * core + c * ROWS, ROWS)
        keep = pltpu.make_async_copy(
            result.at[rows, own_cols, :], o_ref.at[place_rows], out_sems.at[2, c]
        )
        keep.start()
        give = pltpu.make_async_remote_copy(
            src_ref=result.at[rows, away_cols, :], dst_ref=o_ref.at[place_rows],
            send_sem=out_sems.at[0, c], recv_sem=out_sems.at[1, c],
            device_id=sibling, device_id_type=MESH,
        )
        give.start()
        outs += [keep, give]
    wait_all(right_send, 127, right_sems.at[4], right_sems.at[0]).wait_send()
    for c in range(CHUNKS):
        wait_all(left_send.at[c], 127, left_sems.at[0, c], left_sems.at[1, c]).wait_send()
        wait_all(left_send.at[c], 127, tri_sems.at[0, c], tri_sems.at[1, c]).wait_send()
    for out in outs:
        out.wait()


def shards(pair_rep, in_gain, proj_weight, gate_weight, out_gain, out_weight):
    anywhere = pl.BlockSpec(memory_space=pl.ANY)
    return pl.pallas_call(
        kernel,
        out_shape=jax.ShapeDtypeStruct((64, 64, 128), BF16),
        in_specs=[anywhere] * 6,
        out_specs=anywhere,
        scratch_shapes=[
            pltpu.VMEM((64, 64, 128), BF16),
            pltpu.VMEM((1, 128), F32),
            pltpu.VMEM((128, 512), BF16),
            pltpu.VMEM((128, 128), BF16),
            pltpu.VMEM((1, 128), F32),
            pltpu.VMEM((128, 128), BF16),
            pltpu.VMEM((32, 128, 128), BF16),
            pltpu.VMEM((32, 64, 128), BF16),
            pltpu.VMEM((128 * 32, 128), F32),
            pltpu.VMEM((128, 32, 128), BF16),
            pltpu.VMEM((CHUNKS, 128, ROWS, 128), BF16),
            pltpu.VMEM((16, 2, 8, 32, 128), BF16),
            pltpu.VMEM((CHUNKS, 8, 2, 8, ROWS, 128), BF16),
            pltpu.VMEM((CHUNKS, 8, 2, 8, ROWS, 128), BF16),
            pltpu.VMEM((CHUNKS, 128, ROWS, 128), BF16),
            pltpu.VMEM((32, 128, 128), F32),
            pltpu.VMEM((32, 128, 128), BF16),
            pltpu.VMEM((512, 128), BF16),
            pltpu.VMEM((128, 128), F32),
            pltpu.SemaphoreType.REGULAR,
            pltpu.SemaphoreType.REGULAR,
            pltpu.SemaphoreType.DMA((6,)),
            pltpu.SemaphoreType.DMA((2, 4)),
            pltpu.SemaphoreType.DMA((5,)),
            pltpu.SemaphoreType.DMA((1 + 2 * CHUNKS,)),
            pltpu.SemaphoreType.DMA((2, 4)),
            pltpu.SemaphoreType.DMA((2, CHUNKS)),
            pltpu.SemaphoreType.DMA((2, CHUNKS)),
            pltpu.SemaphoreType.DMA((3, CHUNKS)),
        ],
        compiler_params=pltpu.CompilerParams(
            collective_id=0, has_side_effects=True, vmem_limit_bytes=60 * 2**20
        ),
    )(
        pair_rep, in_gain.reshape(1, 128), proj_weight, gate_weight,
        out_gain.reshape(1, 128), out_weight,
    )


def solution(mesh):
    return jax.shard_map(
        shards,
        mesh=mesh,
        in_specs=(P("row", "col", None), P(), P(), P(), P(), P()),
        out_specs=P("row", "col", None),
        check_vma=False,
    )
```

time: 95.8 us -> 87.4 us (0.912)
  Pallas kernels: 90.2 us -> 85 us
  local copies, waits for them, and re-layouts: 5.28 us -> 2.26 us
    pallas_call x1, Pallas kernels: 90.2 us -> 85 us  [shards(): pl.pallas_call(kernel, out_shape=jax.ShapeDtypeStruct((64, 64, 128), BF16...]
    unnamed x13 -> x1, local copies, waits for them, and re-layouts: 5.28 us -> 2.26 us
where the time goes in v2:
time: 87.4 us; the launch traced here: 87.3 us
  Pallas kernels  85 us (97%)
  local copies, waits for them, and re-layouts  2.26 us (3%)
    pallas_call x1, Pallas kernels, shards(): pl.pallas_call(kernel, out_shape=jax.ShapeDtypeStruct((64, 64, 128), BF16...  85 us
    unnamed x1, local copies, waits for them, and re-layouts  2.26 us

profile of v2, /device:TPU:1, one launch (start us, length us, event | category | flops | bytes accessed | tf_op | source)
XLA Modules:
  0.0 87.3 jit_solution(8635355941448865190)
XLA Ops:
  0.0 85.0 %shard_map.64 = bf16[64,64,128]{2,1,0:T(8,128)(2,1)} custom-call(bf16[64,64,128]{2,1,0:T(8,128)(2,1)} %x_hbm.1, f32[1,128]{1,0:T(1,128)} %bitcast.2, bf16[128,512]{1,0:T(8,128)(2,1)} %proj_hbm.1, bf16[128,128]{1,0:T(8,128)(2,1)} %gate_w_hbm.1, f32[1,128]{1,0:T(1,128)} %bitcast.3, bf16[128,128]{1,0:T(8,128)(2,1)} %out_w_hbm.1), custom_call_target="tpu_custom_call" | custom-call | tf_op jit(solution)/shard_map/pallas_call | solution.py:356
  85.0 2.3 %copy.8 = bf16[64,64,128]{2,1,0:T(8,128)(2,1)} copy(bf16[64,64,128]{2,1,0:T(8,128)(2,1)} %shard_map.64) | data formatting | bytes 2097152

commit v3 on v2

--- a/solution.py
+++ b/solution.py
@@ -24,7 +24,7 @@
     x_ref, in_gain_ref, proj_ref, gate_w_ref, out_gain_ref, out_w_ref,
     normed, other, wide, right_send, left_send, right_buf, left_buf,
     tri_send, tri_buf, gates, result, weights_t, gain_cols,
-    ready, ready_core, load_sems, swap_sems, right_sems, own_sems, fwd_sems,
+    ready, load_sems, swap_sems, right_sems, own_sems, fwd_sems,
     left_sems, tri_sems, out_sems,
 ):
     row, col = lax.axis_index("row"), lax.axis_index("col")
@@ -57,16 +57,20 @@
     def greet(device):
         pl.semaphore_signal(barrier, inc=1, device_id=device, device_id_type=MESH)
 
+    def near_z(step):
+        return lax.rem(z + step + step // 4, 8) * 2 + y_lo
+
     def greet_z(step, carry):
-        greet((lax.rem(z + step, 8) * 2 + y_lo, col))
+        greet((near_z(step), col))
         return carry
 
     def greet_plane(step, carry):
         y_lo2, pair2 = plane_at(step)
-        greet((z * 2 + y_lo2, pair2 * 2 + core))
-        return carry
-
-    lax.fori_loop(1, 8, greet_z, 0)
+        for core2 in range(2):
+            greet((z * 2 + y_lo2, pair2 * 2 + core2))
+        return carry
+
+    lax.fori_loop(1, 7, greet_z, 0)
     lax.fori_loop(1, 16, greet_plane, 0)
     greet(sibling)
 
@@ -97,13 +101,19 @@
         return carry
 
     lax.fori_loop(0, 8, norm_away, 0)
-    lax.fori_loop(0, 8, norm_own, 0)
     for load in loads[2:]:
         load.wait()
     weights_t[...] = proj_ref[...].astype(F32).T.astype(BF16)
-    gain_cols[...] = jnp.broadcast_to(out_gain_ref[...], (128, 128)).T
-
-    pl.semaphore_wait(barrier, 23)
+
+    pl.semaphore_wait(barrier, 37)
+
+    def ready_z(step, carry):
+        pl.semaphore_signal(
+            ready, inc=1, device_id=(near_z(step), col), device_id_type=MESH
+        )
+        return carry
+
+    lax.fori_loop(1, 7, ready_z, 0)
     swaps = []
     for part in range(4):
         swap = pltpu.make_async_remote_copy(
@@ -115,13 +125,7 @@
         swap.start()
         swaps.append(swap)
 
-    def ready_z(step, carry):
-        pl.semaphore_signal(
-            ready, inc=1, device_id=(lax.rem(z + step, 8) * 2 + y_lo, col), device_id_type=MESH
-        )
-        return carry
-
-    lax.fori_loop(1, 8, ready_z, 0)
+    lax.fori_loop(0, 8, norm_own, 0)
 
     def project(first_row, part):
         half = weights_t[first_row : first_row + 256, :]
@@ -144,9 +148,7 @@
     for part in range(4):
         swaps[part].wait()
         project(256, part)
-    pl.semaphore_wait(ready, 7)
-    pl.semaphore_signal(ready_core, inc=1, device_id=sibling, device_id_type=MESH)
-    pl.semaphore_wait(ready_core, 1)
+    pl.semaphore_wait(ready, 6)
 
     def send_right(group, carry):
         dz, up2 = 3 - group // 2, lax.rem(up + group + 1, 2)
@@ -223,6 +225,7 @@
 
     own_left = [send_left_chunk(0)]
 
+    gain_cols[...] = jnp.broadcast_to(out_gain_ref[...], (128, 128)).T
     def gate_rows(step, carry):
         first = pl.multiple_of(step * 4, 4)
         rows = normed[pl.ds(first, 4)].reshape(512, 128)
@@ -379,7 +382,6 @@
             pltpu.VMEM((512, 128), BF16),
             pltpu.VMEM((128, 128), F32),
             pltpu.SemaphoreType.REGULAR,
-            pltpu.SemaphoreType.REGULAR,
             pltpu.SemaphoreType.DMA((6,)),
             pltpu.SemaphoreType.DMA((2, 4)),
             pltpu.SemaphoreType.DMA((5,)),

time: 87.4 us -> 87 us (level)
  no operation moved by 1% of the time
where the time goes in v3:
time: 87 us; the launch traced here: 86.9 us
  Pallas kernels  84.6 us (97%)
  local copies, waits for them, and re-layouts  2.26 us (3%)
    pallas_call x1, Pallas kernels, shards(): pl.pallas_call(kernel, out_shape=jax.ShapeDtypeStruct((64, 64, 128), BF16...  84.6 us
    unnamed x1, local copies, waits for them, and re-layouts  2.26 us

profile of v3, /device:TPU:1, one launch (start us, length us, event | category | flops | bytes accessed | tf_op | source)
XLA Modules:
  0.0 86.9 jit_solution(2531222223750074107)
XLA Ops:
  0.0 84.6 %shard_map.64 = bf16[64,64,128]{2,1,0:T(8,128)(2,1)} custom-call(bf16[64,64,128]{2,1,0:T(8,128)(2,1)} %x_hbm.1, f32[1,128]{1,0:T(1,128)} %bitcast.2, bf16[128,512]{1,0:T(8,128)(2,1)} %proj_hbm.1, bf16[128,128]{1,0:T(8,128)(2,1)} %gate_w_hbm.1, f32[1,128]{1,0:T(1,128)} %bitcast.3, bf16[128,128]{1,0:T(8,128)(2,1)} %out_w_hbm.1), custom_call_target="tpu_custom_call" | custom-call | tf_op jit(solution)/shard_map/pallas_call | solution.py:359
  84.6 2.3 %copy.8 = bf16[64,64,128]{2,1,0:T(8,128)(2,1)} copy(bf16[64,64,128]{2,1,0:T(8,128)(2,1)} %shard_map.64) | data formatting | bytes 2097152

commit v4 on v3

--- a/solution.py
+++ b/solution.py
@@ -354,9 +354,28 @@
         out.wait()
 
 
+def place_kernel(src_ref, dst_ref, tiles, sems):
+    parts = [pl.ds(16 * i, 16) for i in range(4)]
+    loads = [
+        pltpu.make_async_copy(src_ref.at[part], tiles.at[part], sems.at[0, i])
+        for i, part in enumerate(parts)
+    ]
+    stores = [
+        pltpu.make_async_copy(tiles.at[part], dst_ref.at[part], sems.at[1, i])
+        for i, part in enumerate(parts)
+    ]
+    for load in loads:
+        load.start()
+    for load, store in zip(loads, stores):
+        load.wait()
+        store.start()
+    for store in stores:
+        store.wait()
+
+
 def shards(pair_rep, in_gain, proj_weight, gate_weight, out_gain, out_weight):
     anywhere = pl.BlockSpec(memory_space=pl.ANY)
-    return pl.pallas_call(
+    update = pl.pallas_call(
         kernel,
         out_shape=jax.ShapeDtypeStruct((64, 64, 128), BF16),
         in_specs=[anywhere] * 6,
@@ -398,6 +417,17 @@
         pair_rep, in_gain.reshape(1, 128), proj_weight, gate_weight,
         out_gain.reshape(1, 128), out_weight,
     )
+    return pl.pallas_call(
+        place_kernel,
+        out_shape=jax.ShapeDtypeStruct((64, 64, 128), BF16),
+        in_specs=[anywhere],
+        out_specs=anywhere,
+        scratch_shapes=[
+            pltpu.VMEM((64, 64, 128), BF16),
+            pltpu.SemaphoreType.DMA((2, 4)),
+        ],
+        compiler_params=pltpu.CompilerParams(vmem_limit_bytes=60 * 2**20),
+    )(update)
 
 
 def solution(mesh):

time: 87 us -> 86.7 us (level)
  local copies, waits for them, and re-layouts: 2.26 us -> 0 us
  Pallas kernels: 84.6 us -> 86.6 us
    unnamed x1 -> x0, local copies, waits for them, and re-layouts: 2.26 us -> none
    pallas_call x0 -> x1, Pallas kernels: none -> 1.98 us  [shards(): pl.pallas_call(place_kernel, out_shape=jax.ShapeDtypeStruct((64, 64, 128)...]
where the time goes in v4:
time: 86.7 us; the launch traced here: 86.6 us
  Pallas kernels  86.6 us (100%)
    pallas_call x1, Pallas kernels, shards(): pl.pallas_call(kernel, out_shape=jax.ShapeDtypeStruct((64, 64, 128), BF16...  84.6 us
    pallas_call x1, Pallas kernels, shards(): pl.pallas_call(place_kernel, out_shape=jax.ShapeDtypeStruct((64, 64, 128)...  1.98 us

profile of v4, /device:TPU:1, one launch (start us, length us, event | category | flops | bytes accessed | tf_op | source)
XLA Modules:
  0.0 86.6 jit_solution(6536279176254645126)
XLA Ops:
  0.0 84.6 %shard_map.64.src_ref = bf16[64,64,128]{2,1,0:T(8,128)(2,1)} custom-call(bf16[64,64,128]{2,1,0:T(8,128)(2,1)} %x_hbm.1, f32[1,128]{1,0:T(1,128)} %bitcast.2, bf16[128,512]{1,0:T(8,128)(2,1)} %proj_hbm.1, bf16[128,128]{1,0:T(8,128)(2,1)} %gate_w_hbm.1, f32[1,128]{1,0:T(1,128)} %bitcast.3, bf16[128,128]{1,0:T(8,128)(2,1)} %out_w_hbm.1), custom_call_target="tpu_custom_call" | custom-call | tf_op jit(solution)/shard_map/pallas_call | solution.py:378
  84.6 2.0 %shard_map.65 = bf16[64,64,128]{2,1,0:T(8,128)(2,1)} custom-call(bf16[64,64,128]{2,1,0:T(8,128)(2,1)} %shard_map.64.src_ref), custom_call_target="tpu_custom_call" | custom-call | tf_op jit(solution)/shard_map/pallas_call | solution.py:420
